TPU v7x, 256 devices: a whole 4x4x8 slice. The times are simulated.
256 devices in a mesh: pair: 64 (over y, z_hi, x, core), tok: 4 (over z_lo).
Axes of the slice: x: 4, y: 4, z: 8 (z_hi: 2, z_lo: 4; z = z_hi * 4 + z_lo), core: 2. Of those that a mesh axis runs over, the one named last changes fastest.
Arguments:
- act_vals: bfloat16 [11, 128, 128], P(None, 'tok'), may hold values from 0.5 to 3
- act_idx: int32 [11, 128, 128], replicated, may hold values from 0 to 2047, all different within a row
- slot_pairs: int32 [128, 2], replicated, may hold values from -1 to 10, as said below
- decoders: bfloat16 [128, 2048, 4096], P('pair', None, 'tok'), may hold values from -0.5 to 0.5
- targets: bfloat16 [11, 128, 4096], P(None, 'pair', 'tok'), may hold values from -6 to 6
Outputs:
- feat_grad: float32 [11, 128, 128], P(None, 'pair')
Inputs may be any that keep to these rules, and one draw needn't show every extreme that they name: `slot_pairs`: row 2 * i + j is slot j of index i of pair. A live slot holds a source layer and a target layer with source <= target; exactly 64 slots are live and their pairs are distinct; an empty slot holds -1 in both columns. Some index of pair has all of its 2 slots live. `act_idx`: the 128 feature numbers of one layer and token are distinct.
All inputs are finite; a program needn't handle non-finite values.
Results may differ from a plain program's by a relative error of at most 0.00056.
Values may be sent and summed in bfloat16 or wider, within the bound.
A program may use at most 64 MiB of HBM per device.

v0:
```python
import jax
import jax.numpy as jnp
from jax import lax
from jax.sharding import PartitionSpec as P

D = 4096


def densify(values, positions, feature_count):
    slot_total, row_total, _ = values.shape
    slot_ids = jnp.arange(slot_total)[:, None, None]
    row_ids = jnp.arange(row_total)[None, :, None]
    empty_rows = jnp.zeros((slot_total, row_total, feature_count), jnp.bfloat16)
    return empty_rows.at[slot_ids, row_ids, positions].set(values)


def slot_grads(chosen, decoders, positions):
    gradient = jnp.einsum("srd,sfd->srf", chosen, decoders, preferred_element_type=jnp.float32)
    return jnp.take_along_axis(gradient, positions, axis=2)


def local(act_vals, act_idx, slot_pairs, decoders, targets):
    slots_here = decoders.shape[0]
    feature_count = decoders.shape[1]
    layers = targets.shape[0]
    device = lax.axis_index("pair")
    my_slots = lax.dynamic_slice_in_dim(slot_pairs, device * slots_here, slots_here, 0)
    source_here = jnp.maximum(my_slots[:, 0], 0)
    target_here = jnp.maximum(my_slots[:, 1], 0)
    source_values = jnp.take(act_vals, source_here, axis=0)
    source_positions = jnp.take(act_idx, source_here, axis=0)
    positions = source_positions
    dense_rows = densify(
        lax.all_gather(source_values, "tok", axis=1, tiled=True), positions, feature_count
    )
    partial_value = jnp.einsum(
        "srf,sfd->srd", dense_rows, decoders, preferred_element_type=jnp.float32
    )
    layer_ids = jnp.arange(layers)
    from_source = (slot_pairs[:, 0][:, None] == layer_ids[None, :]).astype(jnp.float32)
    mine_to_target = (my_slots[:, 1][:, None] == layer_ids[None, :]).astype(jnp.float32)
    layer_terms = jnp.einsum(
        "jl,jnd->lnd", mine_to_target, partial_value, precision=lax.Precision.HIGHEST
    )
    rebuilt = lax.psum_scatter(layer_terms, "pair", scatter_dimension=1, tiled=True)
    residual = ((rebuilt - targets.astype(jnp.float32)) * D ** (-0.5)).astype(jnp.bfloat16)
    chosen = jnp.take(lax.all_gather(residual, "pair", axis=1, tiled=True), target_here, axis=0)
    positions = source_positions
    picked = slot_grads(chosen, decoders, positions)
    summed = lax.psum(picked, "tok")
    sorted_in = lax.all_to_all(summed, "pair", split_axis=1, concat_axis=0, tiled=True)
    result = jnp.einsum("jl,jnk->lnk", from_source, sorted_in, precision=lax.Precision.HIGHEST)
    return result


def solution(mesh):
    return jax.shard_map(
        local,
        mesh=mesh,
        in_specs=(P(None, "tok", None), P(), P(), P("pair", None, "tok"), P(None, "pair", "tok")),
        out_specs=P(None, "pair", None),
        check_vma=False,
    )
```

profile of v0, /device:TPU:1, one launch (start us, length us, event | category | flops | bytes accessed | tf_op | source)
XLA Modules:
  0.0 1578.4 jit_solution(8141522395812545311)
XLA Ops:
  6.5 0.8 constant_dynamic-slice_fusion
  7.4 0.3 copy-done
  7.7 0.6 gather_fusion
  8.2 0.1 shift-left_or_fusion
  8.4 0.8 multiply_reduce_fusion
  9.2 0.8 and_reduce_fusion
  10.0 1.4 gather_fusion.1
  11.4 0.1 broadcast_select_fusion.1
  11.5 12.6 all_gather.6
  24.1 224.9 %scatter_custom_fusion = bf16[524288]{0:T(1024)(128)(2,1)S(1)} fusion(s32[32768]{0:T(1024)S(1)} %bitcast.42, bf16[32768]{0:T(1024)(128)(2,1)S(1)} %bitcast.43, bf16[]{:T(256)} %constant.79.clone.1), kind=kCustom, calls=%fused_computation.7 | custom fusion | bytes 1048578
  249.0 0.5 reshape.40
  249.5 4.6 fusion.20
  254.2 4.5 fusion
  258.7 5.9 copy.17
  264.7 0.0 all-gather.2.cloned.1.call-start
  264.7 0.6 dynamic-slice
  266.0 804.5 %all-reduce.6.cloned.1.call-done = f32[11,128,1024]{2,1,0:T(8,128)} async-done(((f32[11,128,1024]{2,1,0:T(8,128)}), f32[11,128,1024]{2,1,0:T(8,128)}) %all-reduce.6.cloned.1.call-update) | async-done | bytes 5767184
  1070.4 1.1 fusion.9
  1071.5 0.6 copy.18
  1072.2 0.3 all-reduce.4.cloned.1.call-start
  1072.4 95.6 %all-gather.2.cloned.1.call-done = bf16[11,128,1024]{2,0,1:T(8,128)(2,1)} async-done(((bf16[11,2,1024]{2,0,1:T(8,128)(2,1)}), bf16[11,128,1024]{2,0,1:T(8,128)(2,1)}) %all-gather.2.cloned.1.call-update) | async-done | bytes 2883600 | tf_op jit(solution)/shard_map/all_gather | solution.py:47
  1168.0 5.5 copy.19
  1173.5 2.4 gather_fusion.2
  1175.9 6.3 fusion.4
  1182.2 321.5 %gather_fusion.3 = f32[32768]{0:T(1024)S(1)} fusion(f32[2,128,2048]{2,1,0:T(8,128)S(1)} %fusion.4, s32[32768]{0:T(1024)S(1)} %bitcast.38), kind=kCustom, calls=%fused_computation.3 | custom fusion | bytes 655360 | tf_op jit(solution)/shard_map/jit(take_along_axis)/gather | solution.py:19
  1503.7 0.8 and_select_fusion
  1504.5 40.0 %all-reduce.4.cloned.1.call-done = f32[2,128,128]{2,1,0:T(8,128)} async-done(((f32[2,128,128]{2,1,0:T(8,128)}), f32[2,128,128]{2,1,0:T(8,128)}) %all-reduce.4.cloned.1.call-update) | async-done | bytes 131088 | tf_op jit(solution)/shard_map/psum | solution.py:50
  1544.5 1.7 copy.20
  1546.1 12.5 all-to-all-start
  1558.6 12.5 all-to-all-done
  1571.1 0.2 fusion.11
  1571.3 0.6 copy.22
  (24 shorter events, 0.2 us)
Async XLA Ops:
  6.5 1.1 copy-start
  6.5 1063.9 %all-reduce.6.cloned.1.call-start = ((), (), s32[]{:S(2)}) async-start(), calls=%async_computation.3 | async-start | bytes 11534336
  8.2 15.9 %copy-start.1 = (s32[2,128,128]{2,1,0:T(8,128)}, s32[2,128,128]{2,1,0:T(8,128)S(1)}, u32[]{:S(2)}) copy-start(s32[2,128,128]{2,1,0:T(8,128)S(1)} %gather_fusion) | copy-start | bytes 393220
  258.7 6.0 copy-start.5
  258.7 811.7 %copy-start.3 = (bf16[11,2,1024]{2,1,0:T(2,128)(2,1)S(1)}, bf16[11,2,1024]{2,1,0:T(2,128)(2,1)}, u32[]{:S(2)}) copy-start(bf16[11,2,1024]{2,1,0:T(2,128)(2,1)} %param.9) | copy-start | bytes 135172
  264.7 903.4 %all-gather.2.cloned.1.call-start = ((), (), s32[]{:S(2)}) async-start(), calls=%async_computation.1 | async-start | bytes 4259840 | tf_op jit(solution)/shard_map/all_gather | solution.py:47
  1072.2 472.3 %all-reduce.4.cloned.1.call-start = ((), (), s32[]{:S(2)}) async-start(), calls=%async_computation.2 | async-start | bytes 262144 | tf_op jit(solution)/shard_map/psum | solution.py:50
  1182.2 321.5 %copy-start.2 = (s32[2,128,128]{2,1,0:T(8,128)S(1)}, s32[2,128,128]{2,1,0:T(8,128)}, u32[]{:S(2)}) copy-start(s32[2,128,128]{2,1,0:T(8,128)} %copy-done.1) | copy-start | bytes 393220
  1182.2 376.4 %copy-start.4 = (s32[128,2]{0,1:T(2,128)S(1)}, s32[128,2]{0,1:T(2,128)}, u32[]{:S(2)}) copy-start(s32[128,2]{0,1:T(2,128)} %param.7) | copy-start | bytes 3076
  1546.1 25.0 %all-to-all-start = ((f32[2,128,128]{2,0,1:T(2,128)}), f32[2,128,128]{2,0,1:T(2,128)S(1)}, u32[]{:S(2)}, u32[]{:S(2)}) async-start(f32[2,128,128]{2,0,1:T(2,128)} %copy.20), calls=%async_computation | async-start | bytes 262144 | tf_op jit(solution)/shard_map/all_to_all | solution.py:51
Sparse Core Ops, SparseCore 0:
  264.8 805.5 all-reduce.5
  1074.0 93.9 all-gather.1
  1504.6 39.8 all-reduce.3
where the time goes:
time: 1580 us
  waiting for transfers between devices  953 us (60%)
  local copies, waits for them, and re-layouts  567 us (36%)
    unnamed x4, waiting for transfers between devices  805 us
    gather x1, local copies, waits for them, and re-layouts, slot_grads(): return jnp.take_along_axis(gradient, positions, axis=2)  321 us
    unnamed x14, local copies, waits for them, and re-layouts  226 us
    all_gather x1, waiting for transfers between devices, local(): lax.all_gather(residual, 'pair', axis=1, tiled=True)  95.6 us
    psum x1, waiting for transfers between devices, local(): summed = lax.psum(picked, 'tok')  40 us
  transfers between devices with their start and end apart: 4, of which 4 were waited for; matrix products, arithmetic and copies ran while one was open for 0% of the time, Pallas kernels for 0%

commit v1 on v0

v1 whole, which is shorter than its diff:
```python
import functools

import jax
import jax.numpy as jnp
from jax import lax
from jax.experimental import pallas as pl
from jax.experimental.pallas import tpu as pltpu
from jax.sharding import PartitionSpec as P

MESH = pl.DeviceIdType.MESH
F32, BF16 = jnp.float32, jnp.bfloat16
L, K, F, D = 11, 128, 2048, 4096
DC = 1024
ROWS = 128
CB = 256
RB = 16


def pair_of(y, zh, x, c):
    return ((y * 2 + zh) * 4 + x) * 2 + c


def kernel(sp, vals, idx, dec_hbm, tg, out, dec, v0, i0, vp, lo, hi, onehot, dense, part, arrived, tgr,
           sums, sums_z, resid, back, grad_in, picked, gsend, grecv, fin, fin_r,
           dec_sem, send_sem, recv_sem):
    pair, tok = lax.axis_index("pair"), lax.axis_index("tok")
    y, zh, x, c = pair // 16, (pair // 8) % 2, (pair // 2) % 4, pair % 2

    def peer(k):
        return (y + k // 8) % 4, (x + (k // 2) % 4) % 4, (c + k) % 2

    def giver(k):
        return (y + 4 - k // 8) % 4, (x + 4 - (k // 2) % 4) % 4, (c + k) % 2

    def remote(src, dst, n, device):
        return pltpu.make_async_remote_copy(src_ref=src, dst_ref=dst, send_sem=send_sem.at[n],
                                            recv_sem=recv_sem.at[n], device_id=device, device_id_type=MESH)

    def dec_copy(j):
        return pltpu.make_async_copy(dec_hbm.at[j], dec.at[j], dec_sem.at[j])

    dec_copy(0).start()
    dec_copy(1).start()

    barrier = pltpu.get_barrier_semaphore()

    def greet(k, _):
        py, px, pc = peer(k)
        pl.semaphore_signal(barrier, inc=1, device_id=(pair_of(py, zh, px, pc), tok), device_id_type=MESH)
        return 0

    lax.fori_loop(1, 32, greet, 0)

    def greet_column(m, _):
        pz, pt = (zh + m // 4) % 2, (tok + m) % 4
        pl.semaphore_signal(barrier, inc=1, device_id=(pair_of(y, pz, x, c), pt), device_id_type=MESH)
        return 0

    lax.fori_loop(1, 8, greet_column, 0)

    for j in range(2):
        layer = jnp.maximum(sp[0, 2 * pair + j], 0)
        v0[j, pl.ds(pl.multiple_of(tok * 32, 32), 32), :] = vals[layer]
        i0[j] = idx[layer]
    pl.semaphore_wait(barrier, 38)

    mine = pl.ds(pl.multiple_of(tok * 32, 32), 32)
    for d in range(1, 4):
        remote(v0.at[:, mine], v0.at[:, mine], 0, (pair, (tok + d) % 4)).start()

    def send_targets(px, _):
        cols = pl.ds(px * 2, 2)
        here = jnp.logical_and(px == x, c == zh)

        @pl.when(jnp.logical_not(here))
        def _():
            remote(tg.at[cols], tgr.at[x * 2 + c], 1, (pair_of(y, zh, px, zh), tok)).start()

        @pl.when(here)
        def _():
            tgr[x * 2 + c] = tg[cols]

        return 0

    lax.fori_loop(0, 4, send_targets, 0)

    pltpu.make_async_remote_copy(src_ref=v0.at[:, pl.ds(0, 96)], dst_ref=v0.at[:, pl.ds(0, 96)],
                                 send_sem=send_sem.at[0], recv_sem=recv_sem.at[0],
                                 device_id=(pair, (tok + 1) % 4), device_id_type=MESH).wait_recv()

    for j in range(2):
        vp[...] = v0[j].astype(F32)
        for gb in range(16):
            g, b = gb // 2, gb % 2
            rows = i0[j, pl.ds(g * 16 + b, 8, stride=2), :]
            lo[j, gb * 8:gb * 8 + 8, :] = jnp.bitwise_and(rows, 127)
            hi[j, gb * 8:gb * 8 + 8, :] = lax.shift_right_logical(rows, 7)

        def two_rows(i, _):
            lefts, rights = [], []
            for u in range(2):
                r = i * 2 + u
                n = (r // 16) * 16 + (r % 8) * 2 + (r // 8) % 2
                low = jnp.broadcast_to(lo[j, pl.ds(r, 1), :], (128, K))
                high = jnp.broadcast_to(hi[j, pl.ds(r, 1), :], (16, K))
                value = jnp.broadcast_to(vp[pl.ds(n, 1), :], (16, K))
                rights.append(jnp.where(low == lax.broadcasted_iota(jnp.int32, (128, K), 0), 1.0, 0.0).astype(BF16))
                lefts.append(jnp.where(high == lax.broadcasted_iota(jnp.int32, (16, K), 0), value, 0.0).astype(BF16))
            nothing = jnp.zeros((16, K), BF16)
            left = jnp.concatenate([jnp.concatenate([lefts[0], nothing], 1),
                                    jnp.concatenate([nothing, lefts[1]], 1)], 0)
            right = jnp.concatenate(rights, 1)
            onehot[pl.ds(pl.multiple_of(i * 32, 32), 32), :] = lax.dot_general(
                left, right, (((1,), (1,)), ((), ())), preferred_element_type=F32)
            return 0

        lax.fori_loop(0, 64, two_rows, 0)
        for h in range(16):
            dense[j, :, h * 128:h * 128 + 128] = onehot[pl.ds(h, ROWS, stride=16), :].astype(BF16)

        dec_copy(j).wait()

        def column_block(i, _):
            px = (x + i) % 4
            part[j, px] = jnp.dot(dense[j], dec[j, :, pl.ds(pl.multiple_of(px * CB, CB), CB)],
                                  preferred_element_type=F32)

            def send_block(m, _):
                py, pc = (y + m // 2) % 4, (c + m) % 2
                k = ((m // 2) * 4 + i) * 2 + m % 2
                rows = pl.ds(pl.multiple_of((py * 2 + pc) * RB, RB), RB)

                @pl.when(k != 0)
                def _():
                    remote(part.at[j, px, rows], arrived.at[j, k], 2 + j, (pair_of(py, zh, px, pc), tok)).start()

                @pl.when(k == 0)
                def _():
                    arrived[j, k] = part[j, px, rows, :]

                return 0

            lax.fori_loop(0, 8, send_block, 0)
            return 0

        lax.fori_loop(0, 4, column_block, 0)

    for l in range(L):
        sums[l] = jnp.zeros((RB, CB), F32)

    @pl.when(c == zh)
    def _():
        wait_blocks = pltpu.make_async_remote_copy(
            src_ref=tgr.at[pl.ds(0, 7)], dst_ref=tgr.at[pl.ds(0, 7)], send_sem=send_sem.at[1],
            recv_sem=recv_sem.at[1], device_id=(pair, (tok + 1) % 4), device_id_type=MESH)
        wait_blocks.wait_recv()

        def minus(l, _):
            for b in range(2):
                for q in range(2):
                    sums[l, b * 8:b * 8 + 8, q * 128:q * 128 + 128] = -tgr.reshape(8 * 48, 128)[
                        pl.ds(q * 24 + l * 2 + b, 8, stride=48), :]
            return 0

        lax.fori_loop(0, L, minus, 0)

    for j in range(2):
        blocks = arrived.at[j, pl.ds(1, 31)]
        pltpu.make_async_remote_copy(src_ref=blocks, dst_ref=blocks, send_sem=send_sem.at[2 + j],
                                     recv_sem=recv_sem.at[2 + j], device_id=(pair, (tok + 1) % 4),
                                     device_id_type=MESH).wait_recv()
        for half in range(2):
            def add(k, totals):
                gy, gx, gc = giver(k)
                target = sp[1, 2 * pair_of(gy, zh, gx, gc) + j]
                block = arrived[j, k, half * 8:half * 8 + 8, :]
                return tuple(t + jnp.where(target == l, block, 0.0) for l, t in enumerate(totals))

            totals = lax.fori_loop(0, 32, add, tuple(sums[l, half * 8:half * 8 + 8, :] for l in range(L)))
            for l in range(L):
                sums[l, half * 8:half * 8 + 8, :] = totals[l]

    exchange = remote(sums, sums_z, 4, (pair_of(y, 1 - zh, x, c), tok))
    exchange.start()
    exchange.wait()
    for l in range(L):
        resid[l] = ((sums[l] + sums_z[l]) * D ** (-0.5)).astype(BF16)

    my_rows = pl.ds(pl.multiple_of((y * 2 + c) * RB, RB), RB)
    my_cols = pl.ds(pl.multiple_of(x * CB, CB), CB)
    for j in range(2):
        def give_back(k, _):
            py, px, pc = peer(k)
            to = pair_of(py, zh, px, pc)
            back[j, k] = resid[jnp.maximum(sp[1, 2 * to + j], 0)]

            @pl.when(k != 0)
            def _():
                remote(back.at[j, k], grad_in.at[j, my_rows, my_cols], 5 + j, (to, tok)).start()

            return 0

        lax.fori_loop(0, 32, give_back, 0)
        grad_in[j, my_rows, my_cols] = back[j, 0]

    for j in range(2):
        blocks = back.at[j, pl.ds(1, 31)]
        pltpu.make_async_remote_copy(src_ref=blocks, dst_ref=blocks, send_sem=send_sem.at[5 + j],
                                     recv_sem=recv_sem.at[5 + j], device_id=(pair, (tok + 1) % 4),
                                     device_id_type=MESH).wait_recv()
        picked[...] = jnp.zeros((ROWS, K), F32)

        def features(f, _):
            grads = lax.dot_general(grad_in[j], dec[j, pl.ds(pl.multiple_of(f * 256, 256), 256), :],
                                    (((1,), (1,)), ((), ())), preferred_element_type=F32)
            for q in range(2):
                chosen = jnp.take_along_axis(grads[:, q * 128:q * 128 + 128], lo[j], axis=1)
                picked[...] = jnp.where(hi[j] == f * 2 + q, chosen, picked[...])
            return 0

        lax.fori_loop(0, 8, features, 0)
        for gb in range(16):
            start = (gb // 4) * 64 + j * 4 + gb % 4
            gsend.reshape(256, K)[pl.ds(start, 8, stride=8), :] = picked[gb * 8:gb * 8 + 8, :]

    def send_picked(k, _):
        py, px, pc = peer(k)
        q = (py * 4 + px) * 2 + pc

        @pl.when(k != 0)
        def _():
            remote(gsend.at[q], grecv.at[k], 7, (pair_of(py, zh, px, pc), tok)).start()

        @pl.when(k == 0)
        def _():
            grecv[k] = gsend[q]

        return 0

    lax.fori_loop(0, 32, send_picked, 0)
    blocks = grecv.at[pl.ds(1, 31)]
    pltpu.make_async_remote_copy(src_ref=blocks, dst_ref=blocks, send_sem=send_sem.at[7], recv_sem=recv_sem.at[7],
                                 device_id=(pair, (tok + 1) % 4), device_id_type=MESH).wait_recv()

    def add_picked(k, totals):
        gy, gx, gc = giver(k)
        first = 2 * pair_of(gy, zh, gx, gc)
        upper = lax.broadcasted_iota(jnp.int32, (8, K), 0) < 4
        source = jnp.where(upper, sp[0, first], sp[0, first + 1])
        block = grecv[k]
        return tuple(t + jnp.where(source == l, block, 0.0) for l, t in enumerate(totals))

    totals = lax.fori_loop(0, 32, add_picked, tuple(jnp.zeros((8, K), F32) for _ in range(L)))
    for l in range(L):
        both = totals[l][0:4] + totals[l][4:8]
        fin[0, 2 * l:2 * l + 2, :] = both[0:2]
        fin[1, 2 * l:2 * l + 2, :] = both[2:4]
    for z in range(2):
        fin[z, 22:24, :] = jnp.zeros((2, K), F32)

    me = zh * 4 + tok

    def send_final(m, _):
        pz, pt = (zh + m // 4) % 2, (tok + m) % 4
        remote(fin.at[pz], fin_r.at[me], 8, (pair_of(y, pz, x, c), pt)).start()
        return 0

    lax.fori_loop(1, 8, send_final, 0)
    fin_r[me] = fin[zh]
    blocks = fin_r.at[pl.ds(0, 7)]
    pltpu.make_async_remote_copy(src_ref=blocks, dst_ref=blocks, send_sem=send_sem.at[8], recv_sem=recv_sem.at[8],
                                 device_id=(pair, (tok + 1) % 4), device_id_type=MESH).wait_recv()
    total = fin_r[0]
    for m in range(1, 8):
        total = total + fin_r[m]
    out[...] = total

    def sent(ref, n):
        pltpu.make_async_remote_copy(src_ref=ref, dst_ref=ref, send_sem=send_sem.at[n], recv_sem=recv_sem.at[n],
                                     device_id=(pair, (tok + 1) % 4), device_id_type=MESH).wait_send()

    sent(v0.at[:, pl.ds(0, 96)], 0)

    @pl.when(c == zh)
    def _():
        sent(tgr.at[pl.ds(0, 3)], 1)

    @pl.when(c != zh)
    def _():
        sent(tgr.at[pl.ds(0, 4)], 1)

    for j in range(2):
        sent(arrived.at[j, pl.ds(1, 31)], 2 + j)
        sent(back.at[j, pl.ds(1, 31)], 5 + j)
    sent(grecv.at[pl.ds(1, 31)], 7)
    sent(fin_r.at[pl.ds(0, 7)], 8)


def local(act_vals, act_idx, slot_pairs, decoders, targets):
    tg = jnp.pad(targets.astype(F32).reshape(2 * L, 8, 128), ((0, 2), (0, 0), (0, 0))).transpose(1, 0, 2)
    vmem = pl.BlockSpec(memory_space=pltpu.VMEM)
    out = pl.pallas_call(
        kernel,
        out_shape=jax.ShapeDtypeStruct((24, K), F32),
        in_specs=[pl.BlockSpec(memory_space=pltpu.SMEM), vmem, vmem, pl.BlockSpec(memory_space=pl.ANY), vmem],
        out_specs=vmem,
        scratch_shapes=[
            pltpu.VMEM((2, F, DC), BF16),
            pltpu.VMEM((2, ROWS, K), BF16),
            pltpu.VMEM((2, ROWS, K), jnp.int32),
            pltpu.VMEM((ROWS, K), F32),
            pltpu.VMEM((2, ROWS, K), jnp.int32),
            pltpu.VMEM((2, ROWS, K), jnp.int32),
            pltpu.VMEM((ROWS * 16, K), F32),
            pltpu.VMEM((2, ROWS, F), BF16),
            pltpu.VMEM((2, 4, ROWS, CB), F32),
            pltpu.VMEM((2, 32, RB, CB), F32),
            pltpu.VMEM((8, 2, 24, 128), F32),
            pltpu.VMEM((L, RB, CB), F32),
            pltpu.VMEM((L, RB, CB), F32),
            pltpu.VMEM((L, RB, CB), BF16),
            pltpu.VMEM((2, 32, RB, CB), BF16),
            pltpu.VMEM((2, ROWS, DC), BF16),
            pltpu.VMEM((ROWS, K), F32),
            pltpu.VMEM((32, 8, K), F32),
            pltpu.VMEM((32, 8, K), F32),
            pltpu.VMEM((2, 24, K), F32),
            pltpu.VMEM((8, 24, K), F32),
            pltpu.SemaphoreType.DMA((2,)),
            pltpu.SemaphoreType.DMA((9,)),
            pltpu.SemaphoreType.DMA((9,)),
        ],
        compiler_params=pltpu.CompilerParams(collective_id=0, has_side_effects=True, vmem_limit_bytes=48 << 20),
        cost_estimate=pl.CostEstimate(flops=2 * 2 * 2 * ROWS * F * DC, bytes_accessed=10 << 20, transcendentals=0),
        name="transcoder",
    )(slot_pairs.T, act_vals, act_idx, decoders, tg)
    return out[:2 * L].reshape(L, 2, K)


def solution(mesh):
    return jax.shard_map(
        local,
        mesh=mesh,
        in_specs=(P(None, "tok", None), P(), P(), P("pair", None, "tok"), P(None, "pair", "tok")),
        out_specs=P(None, "pair", None),
        check_vma=False,
    )
```

time: 1580 us -> 90.6 us (0.06)
  waiting for transfers between devices: 953 us -> 0 us
  local copies, waits for them, and re-layouts: 567 us -> 4.12 us
  Pallas kernels: 0 us -> 86.2 us
    unnamed x4 -> x0, waiting for transfers between devices: 805 us -> none
    gather x4 -> x0, local copies, waits for them, and re-layouts: 326 us -> none  [the longest x1 321 us: slot_grads(): return jnp.take_along_axis(gradient, positions, axis=2)]
    unnamed x14 -> x6, local copies, waits for them, and re-layouts: 226 us -> 2.67 us
    all_gather x1 -> x0, waiting for transfers between devices: 95.6 us -> none  [local(): lax.all_gather(residual, 'pair', axis=1, tiled=True)]
    pallas_call x0 -> x1, Pallas kernels: none -> 86.2 us  [local(): pl.pallas_call(kernel, out_shape=jax.ShapeDtypeStruct((24, K), F32), in_s...]
    psum x1 -> x0, waiting for transfers between devices: 40 us -> none  [local(): summed = lax.psum(picked, 'tok')]
  transfers between devices with their start and end apart: 4 -> 0, of which waited for: 4 -> 0; matrix products, arithmetic and copies ran while one was open for 0% -> 0% of each run, Pallas kernels for 0% -> 0%
where the time goes in v1:
time: 90.6 us; the launch traced here: 90.3 us
  Pallas kernels  86.2 us (95%)
  local copies, waits for them, and re-layouts  4.12 us (5%)
    pallas_call x1, Pallas kernels, local(): pl.pallas_call(kernel, out_shape=jax.ShapeDtypeStruct((24, K), F32), in_s...  86.2 us
    unnamed x6, local copies, waits for them, and re-layouts  2.67 us

profile of v1, /device:TPU:1, one launch (start us, length us, event | category | flops | bytes accessed | tf_op | source)
XLA Modules:
  0.0 90.3 jit_solution(3438295921021591713)
XLA Ops:
  0.0 0.8 reshape.7
  0.9 0.0 copy-start
  0.9 1.1 %copy-done = s32[11,128,128]{2,1,0:T(8,128)S(1)} copy-done((s32[11,128,128]{2,1,0:T(8,128)S(1)}, s32[11,128,128]{2,1,0:T(8,128)}, u32[]{:S(2)}) %copy-start) | copy-done | bytes 720920
  2.0 0.0 copy-start.1
  2.0 0.9 copy-done.1
  2.9 0.0 copy-start.2
  2.9 0.7 copy-done.2
  3.5 86.2 %transcoder.1 = f32[24,128]{1,0:T(8,128)S(1)} custom-call(s32[2,128]{1,0:T(2,128)S(1)} %bitcast.5, bf16[11,32,128]{2,1,0:T(8,128)(2,1)S(1)} %copy-done.1, s32[11,128,128]{2,1,0:T(8,128)S(1)} %copy-done, bf16[2,2048,1024]{2,1,0:T(8,128)(2,1)} %dec_hbm.1, f32[8,24,128]{2,1,0:T(8,128)S(1)} %convert_bitcast_fusion.tg), custom_call_target="tpu_custom_call" | custom-call | flops 2147483648 | bytes 10485760 | tf_op jit(solution)/shard_map/transcoder/pallas_call | solution.py:302
  89.7 0.6 reshape.8
  (2 shorter events, 0.0 us)
Async XLA Ops:
  0.9 1.1 %copy-start = (s32[11,128,128]{2,1,0:T(8,128)S(1)}, s32[11,128,128]{2,1,0:T(8,128)}, u32[]{:S(2)}) copy-start(s32[11,128,128]{2,1,0:T(8,128)} %idx.1) | copy-start | bytes 2162692
  2.0 0.9 copy-start.1
  2.9 0.7 copy-start.2

commit v2 on v0

v2 whole, which is shorter than its diff:
```python
import functools

import jax
import jax.numpy as jnp
from jax import lax
from jax.experimental import pallas as pl
from jax.experimental.pallas import tpu as pltpu
from jax.sharding import PartitionSpec as P

MESH = pl.DeviceIdType.MESH
F32, BF16, I32 = jnp.float32, jnp.bfloat16, jnp.int32
NT = (((1,), (1,)), ((), ()))
L, K, F, D = 11, 128, 2048, 4096
DC = 1024
ROWS = 128
CB = 256
RB = 16
UNROLL = 16


def place_maps(j, lo, hi, onehot, inv):
    nothing = jnp.zeros((16, K), BF16)
    lows = lax.broadcasted_iota(I32, (128, K), 0).astype(F32).astype(BF16)
    highs = lax.broadcasted_iota(I32, (16, K), 0)
    places = lax.broadcasted_iota(I32, (16, K), 1) + 1

    def masks(r):
        low = jnp.broadcast_to(lo[j, pl.ds(r, 1), :].astype(F32).astype(BF16), (128, K))
        high = jnp.broadcast_to(hi[j, pl.ds(r, 1), :], (16, K))
        return (jnp.where(high == highs, places, 0).astype(F32).astype(BF16),
                jnp.where(low == lows, jnp.ones((), BF16), jnp.zeros((), BF16)))

    def rows(i, _):
        for u in range(UNROLL):
            r = i * (2 * UNROLL) + 2 * u
            (left0, right0), (left1, right1) = masks(r), masks(r + 1)
            left = jnp.concatenate([jnp.concatenate([left0, nothing], 1), jnp.concatenate([nothing, left1], 1)], 0)
            onehot[pl.ds(pl.multiple_of(r * 16, 32), 32), :] = lax.dot_general(
                left, jnp.concatenate([right0, right1], 1), NT, preferred_element_type=F32)
        return 0

    lax.fori_loop(0, 64 // UNROLL, rows, 0)
    for h in range(16):
        inv[j, h] = onehot[pl.ds(h, ROWS, stride=16), :].astype(I32)


def kernel(sp_hbm, vals_hbm, idx_hbm, dec_hbm, tg_hbm, out, sp, vals, idx, tg_ref, dec, v0, i0, vp, lo, hi, onehot, inv,
           dense, part, arrived, tg, tgr, sums, sums_z, resid, back, grad_in, picked, gsend, grecv, fin, fin_r,
           loc_sem, send_sem, recv_sem):
    pair, tok = lax.axis_index("pair"), lax.axis_index("tok")
    y, zh, x, c = pair >> 4, (pair >> 3) & 1, (pair >> 1) & 3, pair & 1

    def mate(k):
        return pair ^ (((k & 24) << 1) | (k & 7))

    def remote(src, dst, n, device):
        return pltpu.make_async_remote_copy(src_ref=src, dst_ref=dst, send_sem=send_sem.at[n],
                                            recv_sem=recv_sem.at[n], device_id=device, device_id_type=MESH)

    def whole(ref, n):
        return remote(ref, ref, n, (pair ^ 1, tok))

    leaving = []

    def finish():
        for ref, n in leaving:
            whole(ref, n).wait_send()

    sp_copy = pltpu.make_async_copy(sp_hbm, sp, loc_sem.at[2])
    vals_copy = pltpu.make_async_copy(vals_hbm, vals, loc_sem.at[3])
    idx_copy = pltpu.make_async_copy(idx_hbm, idx, loc_sem.at[4])
    tg_copy = pltpu.make_async_copy(tg_hbm, tg_ref, loc_sem.at[5])
    dec_copy = [pltpu.make_async_copy(dec_hbm.at[j], dec.at[j], loc_sem.at[j]) for j in range(2)]
    sp_copy.start()
    vals_copy.start()
    idx_copy.start()
    tg_copy.start()
    dec_copy[0].start()
    dec_copy[1].start()

    barrier = pltpu.get_barrier_semaphore()

    def greet_column(m, _):
        pl.semaphore_signal(barrier, inc=1, device_id=(pair ^ ((m & 4) << 1), tok ^ (m & 3)), device_id_type=MESH)
        return 0

    lax.fori_loop(1, 8, greet_column, 0)

    def greet(k, _):
        pl.semaphore_signal(barrier, inc=1, device_id=(mate(k), tok), device_id_type=MESH)
        return 0

    lax.fori_loop(1, 32, greet, 0)

    sp_copy.wait()
    idx_copy.wait()
    for j in range(2):
        i0[...] = idx[jnp.maximum(sp[0, 2 * pair + j], 0)]
        for gb in range(16):
            rows = i0[pl.ds((gb // 2) * 16 + gb % 2, 8, stride=2), :]
            lo[j, gb * 8:gb * 8 + 8, :] = jnp.bitwise_and(rows, 127)
            hi[j, gb * 8:gb * 8 + 8, :] = lax.shift_right_logical(rows, 7)
    place_maps(0, lo, hi, onehot, inv)

    tg_copy.wait()
    for b in range(8):
        for l in range(L):
            tg[b, 2 * l:2 * l + 2, :] = tg_ref[l, :, b * 128:b * 128 + 128].astype(F32)
        tg[b, 22:24, :] = jnp.zeros((2, 128), F32)
    mine = pl.ds(pl.multiple_of(tok * 32, 32), 32)
    vals_copy.wait()
    for j in range(2):
        v0[j, mine, :] = vals[jnp.maximum(sp[0, 2 * pair + j], 0)]

    pl.semaphore_wait(barrier, 38)

    for d in range(1, 4):
        remote(v0.at[:, mine], v0.at[:, mine], 0, (pair, tok ^ d)).start()
    leaving.append((v0.at[:, pl.ds(0, 96)], 0))

    def send_targets(i, _):
        px = x ^ i
        cols = pl.ds(px * 2, 2)

        @pl.when(i != 0)
        def _():
            remote(tg.at[cols], tgr.at[x * 2 + c], 1, ((pair & 56) | (px << 1) | zh, tok)).start()

        @pl.when(jnp.logical_and(i == 0, c != zh))
        def _():
            remote(tg.at[cols], tgr.at[x * 2 + c], 1, (pair ^ 1, tok)).start()

        @pl.when(jnp.logical_and(i == 0, c == zh))
        def _():
            tgr[x * 2 + c] = tg[cols]

        return 0

    lax.fori_loop(0, 4, send_targets, 0)
    place_maps(1, lo, hi, onehot, inv)
    whole(v0.at[:, pl.ds(0, 96)], 0).wait_recv()

    for j in range(2):
        vp[...] = v0[j].astype(F32)

        def spread(g, _):
            rows = pl.ds(pl.multiple_of(g * 16, 16), 16)
            values = jnp.concatenate([vp[pl.ds(g * 16 + b, 8, stride=2), :] for b in range(2)], 0)
            for h in range(16):
                place = inv[j, h, rows, :]
                chosen = jnp.take_along_axis(values, jnp.maximum(place - 1, 0), axis=1)
                dense[rows, h * 128:h * 128 + 128] = jnp.where(place > 0, chosen, 0.0).astype(BF16)
            return 0

        lax.fori_loop(0, 8, spread, 0)
        dec_copy[j].wait()

        def column_block(i, _):
            px = x ^ i
            part[j, px] = jnp.dot(dense[...], dec[j, :, pl.ds(pl.multiple_of(px * CB, CB), CB)],
                                  preferred_element_type=F32)

            def send_block(m, _):
                to = pair ^ ((i << 1) | ((m & 6) << 3) | (m & 1))
                rows = pl.ds(pl.multiple_of((((to >> 4) << 1) | (to & 1)) * RB, RB), RB)

                @pl.when((i | m) != 0)
                def _():
                    remote(part.at[j, px, rows], arrived.at[j, i, m], 9 + j * 4 + i, (to, tok)).start()

                @pl.when((i | m) == 0)
                def _():
                    arrived[j, 0, 0] = part[j, px, rows, :]

                return 0

            lax.fori_loop(0, 8, send_block, 0)
            return 0

        lax.fori_loop(0, 4, column_block, 0)
        for i in range(4):
            leaving.append((arrived.at[j, i, pl.ds(0 if i else 1, 8 if i else 7)], 9 + j * 4 + i))

    sums[...] = jnp.zeros((L, RB, CB), F32)

    @pl.when(c == zh)
    def _():
        whole(tgr.at[pl.ds(0, 7)], 1).wait_recv()
        for l in range(L):
            for b in range(2):
                for q in range(2):
                    sums[l, b * 8:b * 8 + 8, q * 128:q * 128 + 128] = -tgr.reshape(8 * 48, 128)[
                        pl.ds(q * 24 + l * 2 + b, 8, stride=48), :]

    for j in range(2):
        for i in range(4):
            whole(arrived.at[j, i, pl.ds(0 if i else 1, 8 if i else 7)], 9 + j * 4 + i).wait_recv()
            for half in range(2):
                def add(m, totals):
                    source = pair ^ ((i << 1) | ((m & 6) << 3) | (m & 1))
                    target = sp[1, 2 * source + j]
                    block = arrived[j, i, m, half * 8:half * 8 + 8, :]
                    return tuple(t + jnp.where(target == l, block, 0.0) for l, t in enumerate(totals))

                totals = lax.fori_loop(0, 8, add, tuple(sums[l, half * 8:half * 8 + 8, :] for l in range(L)),
                                       unroll=2)
                for l in range(L):
                    sums[l, half * 8:half * 8 + 8, :] = totals[l]

    def sent_targets():
        @pl.when(c == zh)
        def _():
            whole(tgr.at[pl.ds(0, 3)], 1).wait_send()

        @pl.when(c != zh)
        def _():
            whole(tgr.at[pl.ds(0, 4)], 1).wait_send()

    exchange = remote(sums, sums_z, 2, (pair ^ 8, tok))
    exchange.start()
    sent_targets()
    exchange.wait()
    for l in range(L):
        resid[l] = ((sums[l] + sums_z[l]) * D ** (-0.5)).astype(BF16)

    my_rows = pl.ds(pl.multiple_of(((y << 1) | c) * RB, RB), RB)
    my_cols = pl.ds(pl.multiple_of(x * CB, CB), CB)
    for j in range(2):
        def give_back(k, _):
            to = mate(k)
            back[j, k] = resid[jnp.maximum(sp[1, 2 * to + j], 0)]
            remote(back.at[j, k], grad_in.at[j, my_rows, my_cols], 3 + j, (to, tok)).start()
            return 0

        lax.fori_loop(1, 32, give_back, 0)
        grad_in[j, my_rows, my_cols] = resid[jnp.maximum(sp[1, 2 * pair + j], 0)]
        leaving.append((back.at[j, pl.ds(1, 31)], 3 + j))

    for j in range(2):
        whole(back.at[j, pl.ds(1, 31)], 3 + j).wait_recv()
        picked[...] = jnp.zeros((ROWS, K), F32)

        def features(f, _):
            grads = lax.dot_general(grad_in[j], dec[j, pl.ds(pl.multiple_of(f * 256, 256), 256), :],
                                    NT, preferred_element_type=F32)
            for q in range(2):
                chosen = jnp.take_along_axis(grads[:, q * 128:q * 128 + 128], lo[j], axis=1)
                picked[...] = jnp.where(hi[j] == f * 2 + q, chosen, picked[...])
            return 0

        lax.fori_loop(0, 8, features, 0)
        for gb in range(16):
            start = (gb // 4) * 64 + j * 4 + gb % 4
            gsend.reshape(256, K)[pl.ds(start, 8, stride=8), :] = picked[gb * 8:gb * 8 + 8, :]

    def send_picked(k, _):
        to = mate(k)
        q = ((to >> 4) << 3) | (to & 7)
        remote(gsend.at[q], grecv.at[k], 5, (to, tok)).start()
        return 0

    lax.fori_loop(1, 32, send_picked, 0)
    grecv[0] = gsend[(y << 3) | (x << 1) | c]
    leaving.append((grecv.at[pl.ds(1, 31)], 5))
    whole(grecv.at[pl.ds(1, 31)], 5).wait_recv()

    def add_picked(k, totals):
        first = 2 * mate(k)
        upper = lax.broadcasted_iota(I32, (8, K), 0) < 4
        source = jnp.where(upper, sp[0, first], sp[0, first + 1])
        block = grecv[k]
        return tuple(t + jnp.where(source == l, block, 0.0) for l, t in enumerate(totals))

    totals = lax.fori_loop(0, 32, add_picked, tuple(jnp.zeros((8, K), F32) for _ in range(L)), unroll=2)
    for l in range(L):
        both = totals[l][0:4] + totals[l][4:8]
        fin[0, 2 * l:2 * l + 2, :] = both[0:2]
        fin[1, 2 * l:2 * l + 2, :] = both[2:4]
    for z in range(2):
        fin[z, 22:24, :] = jnp.zeros((2, K), F32)

    me = (zh << 2) | tok

    def send_final(m, _):
        remote(fin.at[zh ^ (m >> 2)], fin_r.at[me], 6, (pair ^ ((m & 4) << 1), tok ^ (m & 3))).start()
        return 0

    lax.fori_loop(1, 8, send_final, 0)
    fin_r[me] = fin[zh]
    whole(fin_r.at[pl.ds(0, 7)], 6).wait_recv()
    leaving.append((fin_r.at[pl.ds(0, 7)], 6))
    total = fin_r[0]
    for m in range(1, 8):
        total = total + fin_r[m]
    for l in range(L):
        out[l] = total[2 * l:2 * l + 2]
    finish()


def local(act_vals, act_idx, slot_pairs, decoders, targets):
    hbm, vmem = pl.BlockSpec(memory_space=pltpu.HBM), pl.BlockSpec(memory_space=pltpu.VMEM)
    return pl.pallas_call(
        kernel,
        out_shape=jax.ShapeDtypeStruct((L, 2, K), F32),
        in_specs=[hbm] * 5,
        out_specs=vmem,
        scratch_shapes=[
            pltpu.SMEM((2, 128), I32),
            pltpu.VMEM((L, 32, K), BF16),
            pltpu.VMEM((L, ROWS, K), I32),
            pltpu.VMEM((L, 2, DC), BF16),
            pltpu.VMEM((2, F, DC), BF16),
            pltpu.VMEM((2, ROWS, K), BF16),
            pltpu.VMEM((ROWS, K), I32),
            pltpu.VMEM((ROWS, K), F32),
            pltpu.VMEM((2, ROWS, K), I32),
            pltpu.VMEM((2, ROWS, K), I32),
            pltpu.VMEM((ROWS * 16, K), F32),
            pltpu.VMEM((2, 16, ROWS, K), I32),
            pltpu.VMEM((ROWS, F), BF16),
            pltpu.VMEM((2, 4, ROWS, CB), F32),
            pltpu.VMEM((2, 4, 8, RB, CB), F32),
            pltpu.VMEM((8, 24, 128), F32),
            pltpu.VMEM((8, 2, 24, 128), F32),
            pltpu.VMEM((L, RB, CB), F32),
            pltpu.VMEM((L, RB, CB), F32),
            pltpu.VMEM((L, RB, CB), BF16),
            pltpu.VMEM((2, 32, RB, CB), BF16),
            pltpu.VMEM((2, ROWS, DC), BF16),
            pltpu.VMEM((ROWS, K), F32),
            pltpu.VMEM((32, 8, K), F32),
            pltpu.VMEM((32, 8, K), F32),
            pltpu.VMEM((2, 24, K), F32),
            pltpu.VMEM((8, 24, K), F32),
            pltpu.SemaphoreType.DMA((6,)),
            pltpu.SemaphoreType.DMA((17,)),
            pltpu.SemaphoreType.DMA((17,)),
        ],
        compiler_params=pltpu.CompilerParams(collective_id=0, has_side_effects=True, vmem_limit_bytes=60 << 20),
        cost_estimate=pl.CostEstimate(flops=2 * 2 * 2 * ROWS * F * DC, bytes_accessed=10 << 20, transcendentals=0),
        name="transcoder",
    )(slot_pairs.T, act_vals, act_idx, decoders, targets)


def solution(mesh):
    return jax.shard_map(
        local,
        mesh=mesh,
        in_specs=(P(None, "tok", None), P(), P(), P("pair", None, "tok"), P(None, "pair", "tok")),
        out_specs=P(None, "pair", None),
        check_vma=False,
    )
```

time: 1580 us -> 70 us (0.04)
  waiting for transfers between devices: 953 us -> 0 us
  local copies, waits for them, and re-layouts: 567 us -> 1.31 us
  Pallas kernels: 0 us -> 68.5 us
    unnamed x4 -> x0, waiting for transfers between devices: 805 us -> none
    gather x4 -> x0, local copies, waits for them, and re-layouts: 326 us -> none  [the longest x1 321 us: slot_grads(): return jnp.take_along_axis(gradient, positions, axis=2)]
    unnamed x14 -> x1, local copies, waits for them, and re-layouts: 226 us -> 1.31 us
    all_gather x1 -> x0, waiting for transfers between devices: 95.6 us -> none  [local(): lax.all_gather(residual, 'pair', axis=1, tiled=True)]
    pallas_call x0 -> x1, Pallas kernels: none -> 68.5 us  [local(): pl.pallas_call(kernel, out_shape=jax.ShapeDtypeStruct((L, 2, K), F32), in...]
    psum x1 -> x0, waiting for transfers between devices: 40 us -> none  [local(): summed = lax.psum(picked, 'tok')]
  transfers between devices with their start and end apart: 4 -> 0, of which waited for: 4 -> 0; matrix products, arithmetic and copies ran while one was open for 0% -> 0% of each run, Pallas kernels for 0% -> 0%
where the time goes in v2:
time: 70 us; the launch traced here: 69.8 us
  Pallas kernels  68.5 us (98%)
  local copies, waits for them, and re-layouts  1.31 us (2%)
    pallas_call x1, Pallas kernels, local(): pl.pallas_call(kernel, out_shape=jax.ShapeDtypeStruct((L, 2, K), F32), in...  68.5 us

profile of v2, /device:TPU:1, one launch (start us, length us, event | category | flops | bytes accessed | tf_op | source)
XLA Modules:
  0.0 69.8 jit_solution(60684351330219748)
XLA Ops:
  0.0 68.5 %transcoder.1 = f32[11,2,128]{2,1,0:T(2,128)} custom-call(s32[2,128]{1,0:T(2,128)} %bitcast.1, bf16[11,32,128]{2,1,0:T(8,128)(2,1)} %vals_hbm.1, s32[11,128,128]{2,1,0:T(8,128)} %idx_hbm.1, bf16[2,2048,1024]{2,1,0:T(8,128)(2,1)} %dec_hbm.1, bf16[11,2,1024]{2,1,0:T(2,128)(2,1)} %tg_hbm.1), custom_call_target="tpu_custom_call" | custom-call | flops 2147483648 | bytes 10485760 | tf_op jit(solution)/shard_map/transcoder/pallas_call | solution.py:302
  68.5 1.3 %copy.7 = f32[11,2,128]{2,1,0:T(2,128)} copy(f32[11,2,128]{2,1,0:T(2,128)} %transcoder.1) | data formatting | bytes 22528

commit v3 on v2

--- a/solution.py
+++ b/solution.py
@@ -14,6 +14,7 @@
 DC = 1024
 ROWS = 128
 CB = 256
+HB = 128
 RB = 16
 UNROLL = 16
 
@@ -45,7 +46,7 @@
 
 
 def kernel(sp_hbm, vals_hbm, idx_hbm, dec_hbm, tg_hbm, out, sp, vals, idx, tg_ref, dec, v0, i0, vp, lo, hi, onehot, inv,
-           dense, part, arrived, tg, tgr, sums, sums_z, resid, back, grad_in, picked, gsend, grecv, fin, fin_r,
+           dense, dect, part, arrived, tg, tgr, sums, sums_z, resid, back, grad_in, picked, gsend, grecv, fin, fin_r,
            loc_sem, send_sem, recv_sem):
     pair, tok = lax.axis_index("pair"), lax.axis_index("tok")
     y, zh, x, c = pair >> 4, (pair >> 3) & 1, (pair >> 1) & 3, pair & 1
@@ -140,6 +141,22 @@
     place_maps(1, lo, hi, onehot, inv)
     whole(v0.at[:, pl.ds(0, 96)], 0).wait_recv()
 
+    def send_blocks(j, h):
+        def send_block(k, _):
+            i = k >> 3
+            m = k & 7
+            to = pair ^ ((i << 1) | ((m & 6) << 3) | (m & 1))
+            rows = pl.ds(pl.multiple_of((((to >> 4) << 1) | (to & 1)) * RB, RB), RB)
+            block = part.at[j, h, x ^ i, rows]
+            remote(block, arrived.at[j, h, i, m], 9 + (j * 2 + h) * 4 + i, (to, tok)).start()
+            return 0
+
+        lax.fori_loop(1, 32, send_block, 0)
+        arrived[j, h, 0, 0] = part[j, h, x, my_rows, :]
+        for i in range(4):
+            leaving.append((arrived.at[j, h, i, pl.ds(0 if i else 1, 8 if i else 7)], 9 + (j * 2 + h) * 4 + i))
+
+    my_rows = pl.ds(pl.multiple_of(((y << 1) | c) * RB, RB), RB)
     for j in range(2):
         vp[...] = v0[j].astype(F32)
 
@@ -154,58 +171,68 @@
 
         lax.fori_loop(0, 8, spread, 0)
         dec_copy[j].wait()
-
-        def column_block(i, _):
-            px = x ^ i
-            part[j, px] = jnp.dot(dense[...], dec[j, :, pl.ds(pl.multiple_of(px * CB, CB), CB)],
-                                  preferred_element_type=F32)
-
-            def send_block(m, _):
-                to = pair ^ ((i << 1) | ((m & 6) << 3) | (m & 1))
-                rows = pl.ds(pl.multiple_of((((to >> 4) << 1) | (to & 1)) * RB, RB), RB)
-
-                @pl.when((i | m) != 0)
-                def _():
-                    remote(part.at[j, px, rows], arrived.at[j, i, m], 9 + j * 4 + i, (to, tok)).start()
-
-                @pl.when((i | m) == 0)
-                def _():
-                    arrived[j, 0, 0] = part[j, px, rows, :]
-
-                return 0
-
-            lax.fori_loop(0, 8, send_block, 0)
+        for px in range(4):
+            both = jnp.dot(dense[...], dec[j, :, px * CB:px * CB + CB], preferred_element_type=F32)
+            part[j, 0, px] = both[:, :HB]
+            part[j, 1, px] = both[:, HB:]
+        send_blocks(j, 0)
+
+    send_blocks(0, 1)
+    send_blocks(1, 1)
+
+    def turn(j):
+        def block(f, _):
+            cols = pl.ds(pl.multiple_of(f * 256, 256), 256)
+            dect[j, :, cols] = dec[j, cols, :].T
             return 0
 
-        lax.fori_loop(0, 4, column_block, 0)
-        for i in range(4):
-            leaving.append((arrived.at[j, i, pl.ds(0 if i else 1, 8 if i else 7)], 9 + j * 4 + i))
-
-    sums[...] = jnp.zeros((L, RB, CB), F32)
+        lax.fori_loop(0, 8, block, 0)
+
+    sums[...] = jnp.zeros((2, L, RB, HB), F32)
 
     @pl.when(c == zh)
     def _():
         whole(tgr.at[pl.ds(0, 7)], 1).wait_recv()
         for l in range(L):
             for b in range(2):
-                for q in range(2):
-                    sums[l, b * 8:b * 8 + 8, q * 128:q * 128 + 128] = -tgr.reshape(8 * 48, 128)[
-                        pl.ds(q * 24 + l * 2 + b, 8, stride=48), :]
-
-    for j in range(2):
-        for i in range(4):
-            whole(arrived.at[j, i, pl.ds(0 if i else 1, 8 if i else 7)], 9 + j * 4 + i).wait_recv()
-            for half in range(2):
+                for h in range(2):
+                    sums[h, l, b * 8:b * 8 + 8, :] = -tgr.reshape(8 * 48, 128)[
+                        pl.ds(h * 24 + l * 2 + b, 8, stride=48), :]
+
+    turn(0)
+    exchange = [remote(sums.at[h], sums_z.at[h], 2 if h else 7, (pair ^ 8, tok)) for h in range(2)]
+
+    def add_up(h):
+        for j in range(2):
+            for i in range(4):
+                whole(arrived.at[j, h, i, pl.ds(0 if i else 1, 8 if i else 7)],
+                      9 + (j * 2 + h) * 4 + i).wait_recv()
+
                 def add(m, totals):
                     source = pair ^ ((i << 1) | ((m & 6) << 3) | (m & 1))
                     target = sp[1, 2 * source + j]
-                    block = arrived[j, i, m, half * 8:half * 8 + 8, :]
+                    block = arrived[j, h, i, m]
                     return tuple(t + jnp.where(target == l, block, 0.0) for l, t in enumerate(totals))
 
-                totals = lax.fori_loop(0, 8, add, tuple(sums[l, half * 8:half * 8 + 8, :] for l in range(L)),
-                                       unroll=2)
+                totals = lax.fori_loop(0, 8, add, tuple(sums[h, l] for l in range(L)), unroll=2)
                 for l in range(L):
-                    sums[l, half * 8:half * 8 + 8, :] = totals[l]
+                    sums[h, l] = totals[l]
+        exchange[h].start()
+
+    def give_back(h):
+        exchange[h].wait()
+        for l in range(L):
+            resid[h, l] = ((sums[h, l] + sums_z[h, l]) * D ** (-0.5)).astype(BF16)
+        my_cols = pl.ds(pl.multiple_of(x * CB + h * HB, HB), HB)
+        for j in range(2):
+            def give(k, _):
+                to = mate(k)
+                back[j, k, h] = resid[h, jnp.maximum(sp[1, 2 * to + j], 0)]
+                remote(back.at[j, k, h], grad_in.at[j, my_rows, my_cols], 3 + j, (to, tok)).start()
+                return 0
+
+            lax.fori_loop(1, 32, give, 0)
+            grad_in[j, my_rows, my_cols] = resid[h, jnp.maximum(sp[1, 2 * pair + j], 0)]
 
     def sent_targets():
         @pl.when(c == zh)
@@ -216,24 +243,13 @@
         def _():
             whole(tgr.at[pl.ds(0, 4)], 1).wait_send()
 
-    exchange = remote(sums, sums_z, 2, (pair ^ 8, tok))
-    exchange.start()
+    add_up(0)
+    add_up(1)
+    give_back(0)
+    turn(1)
     sent_targets()
-    exchange.wait()
-    for l in range(L):
-        resid[l] = ((sums[l] + sums_z[l]) * D ** (-0.5)).astype(BF16)
-
-    my_rows = pl.ds(pl.multiple_of(((y << 1) | c) * RB, RB), RB)
-    my_cols = pl.ds(pl.multiple_of(x * CB, CB), CB)
-    for j in range(2):
-        def give_back(k, _):
-            to = mate(k)
-            back[j, k] = resid[jnp.maximum(sp[1, 2 * to + j], 0)]
-            remote(back.at[j, k], grad_in.at[j, my_rows, my_cols], 3 + j, (to, tok)).start()
-            return 0
-
-        lax.fori_loop(1, 32, give_back, 0)
-        grad_in[j, my_rows, my_cols] = resid[jnp.maximum(sp[1, 2 * pair + j], 0)]
+    give_back(1)
+    for j in range(2):
         leaving.append((back.at[j, pl.ds(1, 31)], 3 + j))
 
     for j in range(2):
@@ -241,14 +257,14 @@
         picked[...] = jnp.zeros((ROWS, K), F32)
 
         def features(f, _):
-            grads = lax.dot_general(grad_in[j], dec[j, pl.ds(pl.multiple_of(f * 256, 256), 256), :],
-                                    NT, preferred_element_type=F32)
+            grads = jnp.dot(grad_in[j], dect[j, :, pl.ds(pl.multiple_of(f * 256, 256), 256)],
+                            preferred_element_type=F32)
             for q in range(2):
                 chosen = jnp.take_along_axis(grads[:, q * 128:q * 128 + 128], lo[j], axis=1)
                 picked[...] = jnp.where(hi[j] == f * 2 + q, chosen, picked[...])
             return 0
 
-        lax.fori_loop(0, 8, features, 0)
+        lax.fori_loop(0, 8, features, 0, unroll=4)
         for gb in range(16):
             start = (gb // 4) * 64 + j * 4 + gb % 4
             gsend.reshape(256, K)[pl.ds(start, 8, stride=8), :] = picked[gb * 8:gb * 8 + 8, :]
@@ -318,14 +334,15 @@
             pltpu.VMEM((ROWS * 16, K), F32),
             pltpu.VMEM((2, 16, ROWS, K), I32),
             pltpu.VMEM((ROWS, F), BF16),
-            pltpu.VMEM((2, 4, ROWS, CB), F32),
-            pltpu.VMEM((2, 4, 8, RB, CB), F32),
+            pltpu.VMEM((2, DC, F), BF16),
+            pltpu.VMEM((2, 2, 4, ROWS, HB), F32),
+            pltpu.VMEM((2, 2, 4, 8, RB, HB), F32),
             pltpu.VMEM((8, 24, 128), F32),
             pltpu.VMEM((8, 2, 24, 128), F32),
-            pltpu.VMEM((L, RB, CB), F32),
-            pltpu.VMEM((L, RB, CB), F32),
-            pltpu.VMEM((L, RB, CB), BF16),
-            pltpu.VMEM((2, 32, RB, CB), BF16),
+            pltpu.VMEM((2, L, RB, HB), F32),
+            pltpu.VMEM((2, L, RB, HB), F32),
+            pltpu.VMEM((2, L, RB, HB), BF16),
+            pltpu.VMEM((2, 32, 2, RB, HB), BF16),
             pltpu.VMEM((2, ROWS, DC), BF16),
             pltpu.VMEM((ROWS, K), F32),
             pltpu.VMEM((32, 8, K), F32),
@@ -333,8 +350,8 @@
             pltpu.VMEM((2, 24, K), F32),
             pltpu.VMEM((8, 24, K), F32),
             pltpu.SemaphoreType.DMA((6,)),
-            pltpu.SemaphoreType.DMA((17,)),
-            pltpu.SemaphoreType.DMA((17,)),
+            pltpu.SemaphoreType.DMA((25,)),
+            pltpu.SemaphoreType.DMA((25,)),
         ],
         compiler_params=pltpu.CompilerParams(collective_id=0, has_side_effects=True, vmem_limit_bytes=60 << 20),
         cost_estimate=pl.CostEstimate(flops=2 * 2 * 2 * ROWS * F * DC, bytes_accessed=10 << 20, transcendentals=0),

time: 70 us -> 59.6 us (0.85)
  Pallas kernels: 68.5 us -> 58.1 us
    pallas_call x1, Pallas kernels: 68.5 us -> 58.1 us  [local(): pl.pallas_call(kernel, out_shape=jax.ShapeDtypeStruct((L, 2, K), F32), in...]
where the time goes in v3:
time: 59.6 us; the launch traced here: 59.4 us
  Pallas kernels  58.1 us (97%)
  local copies, waits for them, and re-layouts  1.31 us (2%)
    pallas_call x1, Pallas kernels, local(): pl.pallas_call(kernel, out_shape=jax.ShapeDtypeStruct((L, 2, K), F32), in...  58.1 us
    unnamed x1, local copies, waits for them, and re-layouts  1.31 us

profile of v3, /device:TPU:1, one launch (start us, length us, event | category | flops | bytes accessed | tf_op | source)
XLA Modules:
  0.0 59.4 jit_solution(15048546336829822253)
XLA Ops:
  0.0 58.1 %transcoder.1 = f32[11,2,128]{2,1,0:T(2,128)} custom-call(s32[2,128]{1,0:T(2,128)} %bitcast.1, bf16[11,32,128]{2,1,0:T(8,128)(2,1)} %vals_hbm.1, s32[11,128,128]{2,1,0:T(8,128)} %idx_hbm.1, bf16[2,2048,1024]{2,1,0:T(8,128)(2,1)} %dec_hbm.1, bf16[11,2,1024]{2,1,0:T(2,128)(2,1)} %tg_hbm.1), custom_call_target="tpu_custom_call" | custom-call | flops 2147483648 | bytes 10485760 | tf_op jit(solution)/shard_map/transcoder/pallas_call | solution.py:318
  58.1 1.3 %copy.7 = f32[11,2,128]{2,1,0:T(2,128)} copy(f32[11,2,128]{2,1,0:T(2,128)} %transcoder.1) | data formatting | bytes 22528

commit v4 on v3

--- a/solution.py
+++ b/solution.py
@@ -52,7 +52,8 @@
     y, zh, x, c = pair >> 4, (pair >> 3) & 1, (pair >> 1) & 3, pair & 1
 
     def mate(k):
-        return pair ^ (((k & 24) << 1) | (k & 7))
+        bits = (k * 5) & 31
+        return pair ^ (((bits & 24) << 1) | (bits & 7))
 
     def remote(src, dst, n, device):
         return pltpu.make_async_remote_copy(src_ref=src, dst_ref=dst, send_sem=send_sem.at[n],
@@ -101,6 +102,7 @@
             rows = i0[pl.ds((gb // 2) * 16 + gb % 2, 8, stride=2), :]
             lo[j, gb * 8:gb * 8 + 8, :] = jnp.bitwise_and(rows, 127)
             hi[j, gb * 8:gb * 8 + 8, :] = lax.shift_right_logical(rows, 7)
+
     place_maps(0, lo, hi, onehot, inv)
 
     tg_copy.wait()
@@ -138,26 +140,28 @@
         return 0
 
     lax.fori_loop(0, 4, send_targets, 0)
-    place_maps(1, lo, hi, onehot, inv)
-    whole(v0.at[:, pl.ds(0, 96)], 0).wait_recv()
+
+    def group(j, h, i):
+        return arrived.at[j, h, pl.ds(i * 8 if i else 1, 8 if i else 7)]
 
     def send_blocks(j, h):
         def send_block(k, _):
-            i = k >> 3
-            m = k & 7
-            to = pair ^ ((i << 1) | ((m & 6) << 3) | (m & 1))
+            to = mate(k)
             rows = pl.ds(pl.multiple_of((((to >> 4) << 1) | (to & 1)) * RB, RB), RB)
-            block = part.at[j, h, x ^ i, rows]
-            remote(block, arrived.at[j, h, i, m], 9 + (j * 2 + h) * 4 + i, (to, tok)).start()
+            block = part.at[j, h, (to >> 1) & 3, rows]
+            remote(block, arrived.at[j, h, k], 9 + (j * 2 + h) * 4 + (k >> 3), (to, tok)).start()
             return 0
 
         lax.fori_loop(1, 32, send_block, 0)
-        arrived[j, h, 0, 0] = part[j, h, x, my_rows, :]
+        arrived[j, h, 0] = part[j, h, x, my_rows, :]
         for i in range(4):
-            leaving.append((arrived.at[j, h, i, pl.ds(0 if i else 1, 8 if i else 7)], 9 + (j * 2 + h) * 4 + i))
+            leaving.append((group(j, h, i), 9 + (j * 2 + h) * 4 + i))
 
     my_rows = pl.ds(pl.multiple_of(((y << 1) | c) * RB, RB), RB)
     for j in range(2):
+        if j == 0:
+            place_maps(1, lo, hi, onehot, inv)
+            whole(v0.at[:, pl.ds(0, 96)], 0).wait_recv()
         vp[...] = v0[j].astype(F32)
 
         def spread(g, _):
@@ -176,7 +180,6 @@
             part[j, 0, px] = both[:, :HB]
             part[j, 1, px] = both[:, HB:]
         send_blocks(j, 0)
-
     send_blocks(0, 1)
     send_blocks(1, 1)
 
@@ -200,27 +203,31 @@
                         pl.ds(h * 24 + l * 2 + b, 8, stride=48), :]
 
     turn(0)
-    exchange = [remote(sums.at[h], sums_z.at[h], 2 if h else 7, (pair ^ 8, tok)) for h in range(2)]
+    zsem = (7, 2)
 
     def add_up(h):
         for j in range(2):
             for i in range(4):
-                whole(arrived.at[j, h, i, pl.ds(0 if i else 1, 8 if i else 7)],
-                      9 + (j * 2 + h) * 4 + i).wait_recv()
+                whole(group(j, h, i), 9 + (j * 2 + h) * 4 + i).wait_recv()
 
                 def add(m, totals):
-                    source = pair ^ ((i << 1) | ((m & 6) << 3) | (m & 1))
-                    target = sp[1, 2 * source + j]
-                    block = arrived[j, h, i, m]
+                    target = sp[1, 2 * mate(i * 8 + m) + j]
+                    block = arrived[j, h, i * 8 + m]
                     return tuple(t + jnp.where(target == l, block, 0.0) for l, t in enumerate(totals))
 
                 totals = lax.fori_loop(0, 8, add, tuple(sums[h, l] for l in range(L)), unroll=2)
                 for l in range(L):
                     sums[h, l] = totals[l]
-        exchange[h].start()
+
+        def send_layer(l, _):
+            remote(sums.at[h, l], sums_z.at[h, l], zsem[h], (pair ^ 8, tok)).start()
+            return 0
+
+        lax.fori_loop(0, L, send_layer, 0)
+        leaving.append((sums.at[h], zsem[h]))
 
     def give_back(h):
-        exchange[h].wait()
+        whole(sums_z.at[h], zsem[h]).wait_recv()
         for l in range(L):
             resid[h, l] = ((sums[h, l] + sums_z[h, l]) * D ** (-0.5)).astype(BF16)
         my_cols = pl.ds(pl.multiple_of(x * CB + h * HB, HB), HB)
@@ -336,7 +343,7 @@
             pltpu.VMEM((ROWS, F), BF16),
             pltpu.VMEM((2, DC, F), BF16),
             pltpu.VMEM((2, 2, 4, ROWS, HB), F32),
-            pltpu.VMEM((2, 2, 4, 8, RB, HB), F32),
+            pltpu.VMEM((2, 2, 32, RB, HB), F32),
             pltpu.VMEM((8, 24, 128), F32),
             pltpu.VMEM((8, 2, 24, 128), F32),
             pltpu.VMEM((2, L, RB, HB), F32),

time: 59.6 us -> 58.4 us (0.980)
  Pallas kernels: 58.1 us -> 56.9 us
    pallas_call x1, Pallas kernels: 58.1 us -> 56.9 us  [local(): pl.pallas_call(kernel, out_shape=jax.ShapeDtypeStruct((L, 2, K), F32), in...]
where the time goes in v4:
time: 58.4 us; the launch traced here: 58.2 us
  Pallas kernels  56.9 us (97%)
  local copies, waits for them, and re-layouts  1.31 us (2%)
    pallas_call x1, Pallas kernels, local(): pl.pallas_call(kernel, out_shape=jax.ShapeDtypeStruct((L, 2, K), F32), in...  56.9 us
    unnamed x1, local copies, waits for them, and re-layouts  1.31 us

profile of v4, /device:TPU:1, one launch (start us, length us, event | category | flops | bytes accessed | tf_op | source)
XLA Modules:
  0.0 58.2 jit_solution(555252944494968999)
XLA Ops:
  0.0 56.9 %transcoder.1 = f32[11,2,128]{2,1,0:T(2,128)} custom-call(s32[2,128]{1,0:T(2,128)} %bitcast.1, bf16[11,32,128]{2,1,0:T(8,128)(2,1)} %vals_hbm.1, s32[11,128,128]{2,1,0:T(8,128)} %idx_hbm.1, bf16[2,2048,1024]{2,1,0:T(8,128)(2,1)} %dec_hbm.1, bf16[11,2,1024]{2,1,0:T(2,128)(2,1)} %tg_hbm.1), custom_call_target="tpu_custom_call" | custom-call | flops 2147483648 | bytes 10485760 | tf_op jit(solution)/shard_map/transcoder/pallas_call | solution.py:325
  56.9 1.3 %copy.7 = f32[11,2,128]{2,1,0:T(2,128)} copy(f32[11,2,128]{2,1,0:T(2,128)} %transcoder.1) | data formatting | bytes 22528

commit v5 on v4

--- a/solution.py
+++ b/solution.py
@@ -16,7 +16,8 @@
 CB = 256
 HB = 128
 RB = 16
-UNROLL = 16
+UNROLL = 32
+EARLY = 8
 
 
 def place_maps(j, lo, hi, onehot, inv):
@@ -144,7 +145,7 @@
     def group(j, h, i):
         return arrived.at[j, h, pl.ds(i * 8 if i else 1, 8 if i else 7)]
 
-    def send_blocks(j, h):
+    def send_blocks(j, h, first=1, end=32):
         def send_block(k, _):
             to = mate(k)
             rows = pl.ds(pl.multiple_of((((to >> 4) << 1) | (to & 1)) * RB, RB), RB)
@@ -152,7 +153,9 @@
             remote(block, arrived.at[j, h, k], 9 + (j * 2 + h) * 4 + (k >> 3), (to, tok)).start()
             return 0
 
-        lax.fori_loop(1, 32, send_block, 0)
+        lax.fori_loop(first, end, send_block, 0, unroll=4)
+        if end < 32:
+            return
         arrived[j, h, 0] = part[j, h, x, my_rows, :]
         for i in range(4):
             leaving.append((group(j, h, i), 9 + (j * 2 + h) * 4 + i))
@@ -173,14 +176,16 @@
                 dense[rows, h * 128:h * 128 + 128] = jnp.where(place > 0, chosen, 0.0).astype(BF16)
             return 0
 
-        lax.fori_loop(0, 8, spread, 0)
+        lax.fori_loop(0, 8, spread, 0, unroll=4)
         dec_copy[j].wait()
         for px in range(4):
             both = jnp.dot(dense[...], dec[j, :, px * CB:px * CB + CB], preferred_element_type=F32)
             part[j, 0, px] = both[:, :HB]
             part[j, 1, px] = both[:, HB:]
         send_blocks(j, 0)
-    send_blocks(0, 1)
+        if j == 0:
+            send_blocks(0, 1, 1, EARLY)
+    send_blocks(0, 1, EARLY)
     send_blocks(1, 1)
 
     def turn(j):
@@ -238,7 +243,7 @@
                 remote(back.at[j, k, h], grad_in.at[j, my_rows, my_cols], 3 + j, (to, tok)).start()
                 return 0
 
-            lax.fori_loop(1, 32, give, 0)
+            lax.fori_loop(1, 32, give, 0, unroll=4)
             grad_in[j, my_rows, my_cols] = resid[h, jnp.maximum(sp[1, 2 * pair + j], 0)]
 
     def sent_targets():
@@ -282,7 +287,7 @@
         remote(gsend.at[q], grecv.at[k], 5, (to, tok)).start()
         return 0
 
-    lax.fori_loop(1, 32, send_picked, 0)
+    lax.fori_loop(1, 32, send_picked, 0, unroll=4)
     grecv[0] = gsend[(y << 3) | (x << 1) | c]
     leaving.append((grecv.at[pl.ds(1, 31)], 5))
     whole(grecv.at[pl.ds(1, 31)], 5).wait_recv()
@@ -294,7 +299,7 @@
         block = grecv[k]
         return tuple(t + jnp.where(source == l, block, 0.0) for l, t in enumerate(totals))
 
-    totals = lax.fori_loop(0, 32, add_picked, tuple(jnp.zeros((8, K), F32) for _ in range(L)), unroll=2)
+    totals = lax.fori_loop(0, 32, add_picked, tuple(jnp.zeros((8, K), F32) for _ in range(L)), unroll=8)
     for l in range(L):
         both = totals[l][0:4] + totals[l][4:8]
         fin[0, 2 * l:2 * l + 2, :] = both[0:2]

time: 58.4 us -> 57.7 us (0.988)
  Pallas kernels: 56.9 us -> 56.2 us
    pallas_call x1, Pallas kernels: 56.9 us -> 56.2 us  [local(): pl.pallas_call(kernel, out_shape=jax.ShapeDtypeStruct((L, 2, K), F32), in...]
where the time goes in v5:
time: 57.7 us; the launch traced here: 57.5 us
  Pallas kernels  56.2 us (97%)
  local copies, waits for them, and re-layouts  1.31 us (2%)
    pallas_call x1, Pallas kernels, local(): pl.pallas_call(kernel, out_shape=jax.ShapeDtypeStruct((L, 2, K), F32), in...  56.2 us
    unnamed x1, local copies, waits for them, and re-layouts  1.31 us

profile of v5, /device:TPU:1, one launch (start us, length us, event | category | flops | bytes accessed | tf_op | source)
XLA Modules:
  0.0 57.5 jit_solution(16467650955233620665)
XLA Ops:
  0.0 56.2 %transcoder.1 = f32[11,2,128]{2,1,0:T(2,128)} custom-call(s32[2,128]{1,0:T(2,128)} %bitcast.1, bf16[11,32,128]{2,1,0:T(8,128)(2,1)} %vals_hbm.1, s32[11,128,128]{2,1,0:T(8,128)} %idx_hbm.1, bf16[2,2048,1024]{2,1,0:T(8,128)(2,1)} %dec_hbm.1, bf16[11,2,1024]{2,1,0:T(2,128)(2,1)} %tg_hbm.1), custom_call_target="tpu_custom_call" | custom-call | flops 2147483648 | bytes 10485760 | tf_op jit(solution)/shard_map/transcoder/pallas_call | solution.py:330
  56.2 1.3 %copy.7 = f32[11,2,128]{2,1,0:T(2,128)} copy(f32[11,2,128]{2,1,0:T(2,128)} %transcoder.1) | data formatting | bytes 22528

commit v6 on v5

--- a/solution.py
+++ b/solution.py
@@ -106,11 +106,6 @@
 
     place_maps(0, lo, hi, onehot, inv)
 
-    tg_copy.wait()
-    for b in range(8):
-        for l in range(L):
-            tg[b, 2 * l:2 * l + 2, :] = tg_ref[l, :, b * 128:b * 128 + 128].astype(F32)
-        tg[b, 22:24, :] = jnp.zeros((2, 128), F32)
     mine = pl.ds(pl.multiple_of(tok * 32, 32), 32)
     vals_copy.wait()
     for j in range(2):
@@ -122,25 +117,6 @@
         remote(v0.at[:, mine], v0.at[:, mine], 0, (pair, tok ^ d)).start()
     leaving.append((v0.at[:, pl.ds(0, 96)], 0))
 
-    def send_targets(i, _):
-        px = x ^ i
-        cols = pl.ds(px * 2, 2)
-
-        @pl.when(i != 0)
-        def _():
-            remote(tg.at[cols], tgr.at[x * 2 + c], 1, ((pair & 56) | (px << 1) | zh, tok)).start()
-
-        @pl.when(jnp.logical_and(i == 0, c != zh))
-        def _():
-            remote(tg.at[cols], tgr.at[x * 2 + c], 1, (pair ^ 1, tok)).start()
-
-        @pl.when(jnp.logical_and(i == 0, c == zh))
-        def _():
-            tgr[x * 2 + c] = tg[cols]
-
-        return 0
-
-    lax.fori_loop(0, 4, send_targets, 0)
 
     def group(j, h, i):
         return arrived.at[j, h, pl.ds(i * 8 if i else 1, 8 if i else 7)]
@@ -185,6 +161,32 @@
         send_blocks(j, 0)
         if j == 0:
             send_blocks(0, 1, 1, EARLY)
+    tg_copy.wait()
+    for b in range(8):
+        for l in range(L):
+            tg[b, 2 * l:2 * l + 2, :] = tg_ref[l, :, b * 128:b * 128 + 128].astype(F32)
+        tg[b, 22:24, :] = jnp.zeros((2, 128), F32)
+
+    def send_targets(i, _):
+        px = x ^ i
+        cols = pl.ds(px * 2, 2)
+
+        @pl.when(i != 0)
+        def _():
+            remote(tg.at[cols], tgr.at[x * 2 + c], 1, ((pair & 56) | (px << 1) | zh, tok)).start()
+
+        @pl.when(jnp.logical_and(i == 0, c != zh))
+        def _():
+            remote(tg.at[cols], tgr.at[x * 2 + c], 1, (pair ^ 1, tok)).start()
+
+        @pl.when(jnp.logical_and(i == 0, c == zh))
+        def _():
+            tgr[x * 2 + c] = tg[cols]
+
+        return 0
+
+    lax.fori_loop(0, 4, send_targets, 0)
+
     send_blocks(0, 1, EARLY)
     send_blocks(1, 1)
 

time: 57.7 us -> 60.8 us (1.054)
  Pallas kernels: 56.2 us -> 59.3 us
    pallas_call x1, Pallas kernels: 56.2 us -> 59.3 us  [local(): pl.pallas_call(kernel, out_shape=jax.ShapeDtypeStruct((L, 2, K), F32), in...]
where the time goes in v6:
time: 60.8 us; the launch traced here: 60.6 us
  Pallas kernels  59.3 us (98%)
  local copies, waits for them, and re-layouts  1.31 us (2%)
    pallas_call x1, Pallas kernels, local(): pl.pallas_call(kernel, out_shape=jax.ShapeDtypeStruct((L, 2, K), F32), in...  59.3 us
    unnamed x1, local copies, waits for them, and re-layouts  1.31 us

profile of v6, /device:TPU:1, one launch (start us, length us, event | category | flops | bytes accessed | tf_op | source)
XLA Modules:
  0.0 60.6 jit_solution(10044319393350299096)
XLA Ops:
  0.0 59.3 %transcoder.1 = f32[11,2,128]{2,1,0:T(2,128)} custom-call(s32[2,128]{1,0:T(2,128)} %bitcast.1, bf16[11,32,128]{2,1,0:T(8,128)(2,1)} %vals_hbm.1, s32[11,128,128]{2,1,0:T(8,128)} %idx_hbm.1, bf16[2,2048,1024]{2,1,0:T(8,128)(2,1)} %dec_hbm.1, bf16[11,2,1024]{2,1,0:T(2,128)(2,1)} %tg_hbm.1), custom_call_target="tpu_custom_call" | custom-call | flops 2147483648 | bytes 10485760 | tf_op jit(solution)/shard_map/transcoder/pallas_call | solution.py:332
  59.3 1.3 %copy.7 = f32[11,2,128]{2,1,0:T(2,128)} copy(f32[11,2,128]{2,1,0:T(2,128)} %transcoder.1) | data formatting | bytes 22528
